TPU v7x, 256 devices: a whole 4x4x8 slice. The times are simulated.
256 devices in a mesh: cpty: 8 (over z_hi, x), path: 32 (over y, z_lo, core).
Axes of the slice: x: 4, y: 4, z: 8 (z_hi: 2, z_lo: 4; z = z_hi * 4 + z_lo), core: 2. Of those that a mesh axis runs over, the one named last changes fastest.
Arguments:
- exposures: bfloat16 [32768, 8, 4096], P('cpty', None, 'path'), may hold values from 0.099609375 to 2
- defaults: int32 [32768, 4096], P('cpty', 'path'), may hold values from 0 to 8
- base_rate: float32 [32768], P('cpty'), may hold values from 0.05 to 0.6
- loadings: bfloat16 [32768, 64], P('cpty'), may hold values from -1 to 1
- factors: bfloat16 [8, 64, 4096], P(None, None, 'path'), may hold values from -5 to 5
- weights: float32 [8], replicated, may hold values from 0.5 to 1.5
Outputs:
- value: float32 [], replicated
- loading_grad: float32 [32768, 64], P('cpty')
- factor_grad: float32 [8, 64, 4096], P(None, 'cpty', 'path')
All inputs are finite; a program needn't handle non-finite values.
Results may differ from a plain program's by a relative error of at most 0.00045.
Values sent between devices are 32-bit elements; how exact they have to be, the bound alone decides.
A program may use at most 128 MiB of HBM per device.

v0:
```python
import jax
import jax.numpy as jnp
from jax import lax
from jax.sharding import PartitionSpec as P

dt_step = 0.5


def per_device(exposures, defaults, base_rate, loadings, factors, weights):
    dates_count = factors.shape[0]
    factor_count = factors.shape[1]
    paths = lax.axis_size("path") * factors.shape[2]
    cptys = lax.axis_size("cpty") * loadings.shape[0]
    x = jnp.einsum("cf,tfp->ctp", loadings, factors, preferred_element_type=jnp.float32)
    rate = base_rate[:, None, None] * jnp.exp(x)
    hazard = dt_step * jnp.cumsum(rate, axis=1)
    survival = jnp.exp(-hazard)
    dates = jnp.arange(dates_count, dtype=jnp.int32)
    live = (dates[None, :, None] < defaults[:, None, :]).astype(jnp.float32)
    amount = weights[None, :, None] * live * exposures.astype(jnp.float32)
    weighted = amount * survival
    local_total = jnp.sum(weighted)
    grad_rate = -dt_step * jnp.flip(jnp.cumsum(jnp.flip(weighted, 1), axis=1), 1)
    grad_x = (rate * grad_rate).astype(jnp.bfloat16)
    factor_part = jnp.einsum("cf,ctp->tfp", loadings, grad_x, preferred_element_type=jnp.float32)
    factor_grad = lax.psum_scatter(factor_part, "cpty", scatter_dimension=1, tiled=True) * (
        factor_count / cptys
    )
    loads_part = jnp.einsum("ctp,tfp->cf", grad_x, factors, preferred_element_type=jnp.float32)
    loading_grad = lax.psum(loads_part, "path") / paths
    value = lax.psum(local_total, ("cpty", "path")) / (cptys * paths)
    return (value, loading_grad, factor_grad)


def solution(mesh):
    in_specs = (
        P("cpty", None, "path"),
        P("cpty", "path"),
        P("cpty"),
        P("cpty", None),
        P(None, None, "path"),
        P(),
    )
    out_specs = (P(), P("cpty", None), P(None, "cpty", "path"))
    return jax.shard_map(
        per_device, mesh=mesh, in_specs=in_specs, out_specs=out_specs, check_vma=False
    )
```

profile of v0, /device:TPU:1, one launch (start us, length us, event | category | flops | bytes accessed | tf_op | source)
XLA Modules:
  0.0 379.3 jit_solution(7317873577704043302)
XLA Ops:
  8.0 0.0 copy-start
  8.0 0.0 copy-start.4
  8.0 0.0 copy-start.5
  8.0 0.0 copy-start.2
  8.0 0.0 reduce-scatter.2.cloned.1.call-start
  8.1 1.0 copy-done
  9.0 9.0 %fusion.3 = f32[4096,8,128]{2,0,1:T(8,128)} fusion(bf16[8,64,128]{2,1,0:T(8,128)(2,1)} %param.10, bf16[4096,64]{0,1:T(8,128)(2,1)S(1)} %copy-done), kind=kOutput, calls=%fused_computation.9 | convolution fusion | flops 536870912 | bytes 17432576 | tf_op jit(solution)/shard_map/cf,tfp->ctp/dot_general | solution.py:14
  18.0 0.0 copy-done.4
  18.0 0.0 copy-done.5
  18.0 0.0 copy-done.2
  18.0 20.0 %fusion.5 = (f32[]{:T(128)}, f32[4096,8,128]{2,0,1:T(8,128)}) fusion(f32[4096,8,128]{2,0,1:T(8,128)} %fusion.3, f32[4096]{0:T(1024)S(1)} %copy-done.4, bf16[4096,8,128]{2,1,0:T(8,128)(2,1)} %param.6, f32[8]{0:T(128)S(1)} %copy-done.5, s32[4096,128]{1,0:T(8,128)S(1)} %copy-done.2), kind=kOutput, calls=%fused_computation.13 | output fusion | flops 67108864 | bytes 44056612 | tf_op jit(solution)/shard_map/jit(cumsum)/reduce_window_sum | solution.py:16
  38.1 11.2 %rev.7 = f32[4096,8,128]{2,0,1:T(8,128)} reverse(f32[4096,8,128]{2,0,1:T(8,128)} %get-tuple-element.4), dimensions={1} | reverse | bytes 33554432 | tf_op jit(solution)/shard_map/jit(_flip)/rev | solution.py:23
  49.3 12.7 %fusion.6 = f32[4096,8,128]{2,0,1:T(8,128)} fusion(f32[4096,8,128]{2,0,1:T(8,128)} %rev.7), kind=kOutput, calls=%fused_computation.14 | output fusion | flops 29360128 | bytes 33554432 | tf_op jit(solution)/shard_map/jit(cumsum)/reduce_window_sum | solution.py:23
  62.0 0.0 copy-start.3
  62.0 11.8 %multiply_convert_fusion = bf16[4096,8,128]{2,0,1:T(8,128)(2,1)S(1)} fusion(f32[4096,8,128]{2,0,1:T(8,128)} %fusion.6, f32[4096,8,128]{2,0,1:T(8,128)} %fusion.3, f32[4096]{0:T(1024)S(1)} %copy-done.4), kind=kLoop, calls=%fused_computation | loop fusion | flops 16777216 | bytes 41959424 | tf_op jit(solution)/shard_map/convert_element_type | solution.py:24
  73.8 0.0 copy-start.1
  73.8 3.2 copy-done.1
  77.1 2.3 convolution_bitcast_fusion.1
  79.3 0.0 reduce-scatter.2.cloned.1.call-update
  79.3 0.0 all-reduce.2.cloned.1.call-start
  79.4 0.0 copy-done.3
  79.4 7.0 %convolution_bitcast_fusion = f32[4096,64]{0,1:T(8,128)} fusion(bf16[4096,8,128]{2,0,1:T(8,128)(2,1)} %copy-done.1, bf16[8,64,128]{2,1,0:T(8,128)(2,1)S(1)} %copy-done.3), kind=kOutput, calls=%fused_computation.6 | convolution fusion | flops 536870912 | bytes 9568256 | tf_op jit(solution)/shard_map/ctp,tfp->cf/dot_general | solution.py:29
  86.4 0.0 all-reduce.2.cloned.1.call-update
  86.4 82.7 %psum.14 = f32[]{:T(128)} all-reduce(f32[]{:T(128)} %get-tuple-element.3), channel_id=1, replica_groups=mesh['cpty'=8,'path'=32] {'cpty','path'}, use_global_device_ids=true, to_apply=%region_2.3 | all-reduce | flops 1 | bytes 8 | tf_op jit(solution)/shard_map/psum | solution.py:31
  169.7 0.0 reduce-scatter.2.cloned.1.call-done
  169.8 1.4 broadcast_multiply_fusion.1
  171.1 197.3 %all-reduce.2.cloned.1.call-done = f32[4096,64]{0,1:T(8,128)} async-done(((f32[4096,64]{0,1:T(8,128)}), f32[4096,64]{0,1:T(8,128)}) %all-reduce.2.cloned.1.call-update) | async-done | bytes 1048592 | tf_op jit(solution)/shard_map/psum | solution.py:30
  368.5 2.3 broadcast_multiply_fusion
Async XLA Ops:
  8.0 1.0 copy-start
  8.0 10.0 %copy-start.4 = (f32[4096]{0:T(1024)S(1)}, f32[4096]{0:T(1024)}, u32[]{:S(2)}) copy-start(f32[4096]{0:T(1024)} %param.8) | copy-start | bytes 49156
  8.0 10.0 %copy-start.5 = (f32[8]{0:T(128)S(1)}, f32[8]{0:T(128)}, u32[]{:S(2)}) copy-start(f32[8]{0:T(128)} %param.11) | copy-start | bytes 100
  8.0 10.0 %copy-start.2 = (s32[4096,128]{1,0:T(8,128)S(1)}, s32[4096,128]{1,0:T(8,128)}, u32[]{:S(2)}) copy-start(s32[4096,128]{1,0:T(8,128)} %param.7) | copy-start | bytes 6291460
  8.0 161.7 %reduce-scatter.2.cloned.1.call-start = ((), (), s32[]{:S(2)}) async-start(), calls=%async_computation.2 | async-start | bytes 294912 | tf_op jit(solution)/shard_map/reduce_scatter | solution.py:26
  62.0 17.3 %copy-start.3 = (bf16[8,64,128]{2,1,0:T(8,128)(2,1)S(1)}, bf16[8,64,128]{2,1,0:T(8,128)(2,1)}, u32[]{:S(2)}) copy-start(bf16[8,64,128]{2,1,0:T(8,128)(2,1)} %param.10) | copy-start | bytes 393220
  73.8 3.2 copy-start.1
  79.3 289.1 %all-reduce.2.cloned.1.call-start = ((), (), s32[]{:S(2)}) async-start(), calls=%async_computation.1 | async-start | bytes 2097152 | tf_op jit(solution)/shard_map/psum | solution.py:30
Sparse Core Ops, SparseCore 0:
  79.5 85.0 reduce-scatter.1
Sparse Core Ops, SparseCore 1:
  86.5 281.9 all-reduce.1
where the time goes:
time: 380 us; the launch traced here: 379 us
  waiting for transfers between devices  197 us (52%)
  blocking collectives  82.7 us (22%)
  other arithmetic  48.2 us (13%)
  matrix products  18.2 us (5%)
  between operations  17.3 us (5%)
  local copies, waits for them, and re-layouts  15.4 us (4%)
    psum x1, waiting for transfers between devices, per_device(): loading_grad = lax.psum(loads_part, 'path') / paths  197 us
    psum x1, blocking collectives, per_device(): value = lax.psum(local_total, ('cpty', 'path')) / (cptys * paths)  82.7 us
    another operation x1, other arithmetic, per_device(): hazard = dt_step * jnp.cumsum(rate, axis=1)  20 us
    another operation x1, other arithmetic, per_device(): jnp.cumsum(jnp.flip(weighted, 1), axis=1)  12.7 us
    convert_element_type x1, other arithmetic, per_device(): grad_x = (rate * grad_rate).astype(jnp.bfloat16)  11.8 us
    rev x1, local copies, waits for them, and re-layouts, per_device(): jnp.flip(weighted, 1)  11.2 us
    dot_general x1, matrix products, per_device(): jnp.einsum('cf,tfp->ctp', loadings, factors, preferred_element_type=jnp.f...  8.99 us
  transfers between devices with their start and end apart: 2, of which 1 were waited for; matrix products, arithmetic and copies ran while one was open for 2% of the time, Pallas kernels for 0%

commit v1 on v0

v1 whole, which is shorter than its diff:
```python
import functools
import math

import jax
import jax.numpy as jnp
from jax import lax
from jax.experimental import pallas as pl
from jax.experimental.pallas import tpu as pltpu
from jax.sharding import PartitionSpec as P

LOG2E = 1.4426950408889634
F32, BF = jnp.float32, jnp.bfloat16
MESH = pl.DeviceIdType.MESH
V = pltpu.VMEM


def split3(v):
    h = v.astype(BF)
    r = v - h.astype(F32)
    m = r.astype(BF)
    return h, m, (r - m.astype(F32)).astype(BF)


def terms(R, RB, NDMA, e_hbm, d_hbm, b_hbm, lt_hbm, f_hbm, w_ref, lg_ref, fp_ref, v_ref,
          e, d, bv, lt, f, f3, f2, ya, yb, ga, gb, fp, lg, dsem, ssem):
    CT = 4096
    NB = CT // R
    CH = CT // NDMA
    small = [pltpu.make_async_copy(f_hbm, f, ssem.at[0]), pltpu.make_async_copy(lt_hbm, lt, ssem.at[1]),
             pltpu.make_async_copy(b_hbm, bv, ssem.at[2])]
    for c in small:
        c.start()

    def chunk(i):
        s = pl.ds(i * CH, CH)
        return (pltpu.make_async_copy(e_hbm.at[s], e.at[s], dsem.at[0, i]),
                pltpu.make_async_copy(d_hbm.at[s], d.at[s], dsem.at[1, i]))

    for i in range(NDMA):
        for c in chunk(i):
            c.start()
    for c in small:
        c.wait()
    f3[...] = jnp.zeros_like(f3)
    for t in range(8):
        h, m, l = split3(f[t].astype(F32) * LOG2E)
        sl = slice(t * 128, (t + 1) * 128)
        f3[0:64, sl] = h
        f3[128:192, sl] = m
        f3[192:256, sl] = l
        f2[:, sl] = f[t]
    row = lax.broadcasted_iota(jnp.int32, (16, 1024), 0)
    f3[64:80, :] = jnp.where(row < 3, 1.0, 0.0).astype(BF)
    fp[...] = jnp.zeros_like(fp)
    v_ref[...] = jnp.zeros_like(v_ref)
    gb[...] = jnp.zeros_like(gb)
    wneg = [-math.log(2.0) * w_ref[t] for t in range(8)]

    def ydot(j, y):
        cs = pl.ds(pl.multiple_of(j * R, R), R)
        l = lt[:, cs]
        h, m, lo = split3(jnp.log2(bv[:, cs] * (0.5 * LOG2E)))
        row = lax.broadcasted_iota(jnp.int32, (16, R), 0)
        extra = jnp.where(row == 0, h.astype(F32), jnp.where(row == 1, m.astype(F32), jnp.where(row == 2, lo.astype(F32), 0.0))).astype(BF)
        l3 = jnp.concatenate([l, extra, jnp.zeros((48, R), BF), l, l], axis=0)
        y[...] = lax.dot_general(l3, f3[...], (((0,), (0,)), ((), ())), preferred_element_type=F32)

    def elem(j, y, gx):
        acc = None
        for q in range(R // RB):
            r = pl.multiple_of(j * R + q * RB, RB)
            rl = slice(q * RB, (q + 1) * RB)
            dd = d[pl.ds(r, RB), :]
            es = jnp.swapaxes(e[pl.ds(r, RB)], 0, 1).astype(F32)
            rates, wt, hz = [], [], None
            for t in range(8):
                rt = jnp.exp2(y[rl, t * 128:(t + 1) * 128])
                hz = -rt if t == 0 else hz - rt
                s = jnp.exp2(hz)
                a = jnp.where(t < dd, es[t], 0.0) * wneg[t]
                rates.append(rt)
                wt.append(a * s)
            g = None
            for t in range(7, -1, -1):
                g = wt[t] if g is None else g + wt[t]
                gx[rl, t * 128:(t + 1) * 128] = (rates[t] * g).astype(BF)
            for k in range(RB // 8):
                part = g[k * 8:(k + 1) * 8]
                acc = part if acc is None else acc + part
        v_ref[...] += acc

    def de(j, gx):
        cs = pl.ds(pl.multiple_of(j * R, R), R)
        g = gx[...]
        fp[...] += lax.dot_general(lt[:, cs], g, (((1,), (0,)), ((), ())), preferred_element_type=F32)
        lg[:, cs] = lax.dot_general(f2[...], g, (((1,), (1,)), ((), ())), preferred_element_type=F32)

    ydot(0, ya)
    per = CH // (2 * R)

    def body(k, _):
        @pl.when(k % per == 0)
        def _():
            for c in chunk(k // per):
                c.wait()
        j = 2 * k
        ydot(j + 1, yb)
        elem(j, ya, ga)
        de(jnp.maximum(j - 1, 0), gb)
        ydot(jnp.minimum(j + 2, NB - 1), ya)
        elem(j + 1, yb, gb)
        de(j, ga)
        return 0

    lax.fori_loop(0, NB // 2, body, 0)
    de(NB - 1, gb)
    oc = [pltpu.make_async_copy(lg, lg_ref, ssem.at[0]), pltpu.make_async_copy(fp, fp_ref, ssem.at[1])]
    for c in oc:
        c.start()
    for c in oc:
        c.wait()


def own_terms(exposures, defaults, base, lt, factors, weights):
    R, RB, NDMA, CT = 256, 32, 8, 4096
    A = pl.BlockSpec(memory_space=pl.ANY)
    return pl.pallas_call(
        functools.partial(terms, R, RB, NDMA),
        in_specs=[A, A, A, A, A, pl.BlockSpec(memory_space=pltpu.SMEM)],
        out_specs=[A, A, pl.BlockSpec(memory_space=V)],
        out_shape=[jax.ShapeDtypeStruct((64, CT), F32), jax.ShapeDtypeStruct((64, 1024), F32), jax.ShapeDtypeStruct((8, 128), F32)],
        scratch_shapes=[V((CT, 8, 128), BF), V((CT, 128), jnp.int32), V((1, CT), F32), V((64, CT), BF), V((8, 64, 128), BF),
                        V((256, 1024), BF), V((64, 1024), BF), V((R, 1024), F32), V((R, 1024), F32), V((R, 1024), BF), V((R, 1024), BF),
                        V((64, 1024), F32), V((64, CT), F32), pltpu.SemaphoreType.DMA((2, NDMA)), pltpu.SemaphoreType.DMA((3,))],
        compiler_params=pltpu.CompilerParams(vmem_limit_bytes=48 << 20),
    )(exposures, defaults, base, lt, factors, weights)


def sums(NCH, scale_l, scale_f, scale_v, lg, fp, vin, lo_ref, fo_ref, vo_ref,
         cbuf, rbuf, out, fbuf, vc, vbuf, vp, wbuf, tot, s_c, r_c, s_r, r_r, s_a, r_a, s_d, r_d, s_f, r_f, s_v, r_v, s_w, r_w, lsem):
    CW = 4096 // NCH
    Q = CW // 4
    ci, pi = lax.axis_index("cpty"), lax.axis_index("path")
    y, z, k = pi // 8, (pi // 2) % 4, pi % 2
    mate = (ci, pi - k + (1 - k))

    def chip(j):
        yy, zz = (y + j // 4) % 4, (z + j % 4) % 4
        return yy, zz, (ci, yy * 8 + zz * 2 + k)

    def fam(j):
        cc = (ci + j) % 8
        return cc, (cc, pi)

    barrier = pltpu.get_barrier_semaphore()
    for dev in [mate] + [chip(j)[2] for j in range(1, 16)] + [fam(j)[1] for j in range(1, 8)]:
        pl.semaphore_signal(barrier, inc=1, device_id=dev, device_id_type=MESH)
    pl.semaphore_wait(barrier, 23)

    def rc(src, dst, ss, rs, dev):
        return pltpu.make_async_remote_copy(src, dst, ss, rs, device_id=dev, device_id_type=MESH)

    mine = pl.multiple_of(k * 32, 32)
    other = pl.multiple_of(32 - k * 32, 32)

    def cc(i):
        return rc(lg.at[pl.ds(other, 32), pl.ds(i * CW, CW)], cbuf.at[i], s_c.at[i], r_c.at[i], mate)

    def rs(i, j):
        yy, zz, dev = chip(j)
        return rc(cbuf.at[i, pl.ds(pl.multiple_of(yy * 8, 8), 8), pl.ds(pl.multiple_of(zz * Q, Q), Q)], rbuf.at[i, j],
                  s_r.at[i, j], r_r.at[i, j], dev)

    def ag(i, j):
        _, _, dev = chip(j)
        piece = out.at[pl.ds(pl.multiple_of(mine + y * 8, 8), 8), pl.ds(pl.multiple_of(i * CW + z * Q, Q), Q)]
        return rc(piece, piece, s_a.at[i, j], r_a.at[i, j], dev)

    def dd(i):
        half = out.at[pl.ds(mine, 32), pl.ds(i * CW, CW)]
        return rc(half, half, s_d.at[i], r_d.at[i], mate)

    def ff(j):
        cc_, dev = fam(j)
        return rc(fp.at[pl.ds(pl.multiple_of(cc_ * 8, 8), 8)], fbuf.at[j], s_f.at[j], r_f.at[j], dev)

    vcopy = rc(vin, vc, s_v.at[0], r_v.at[0], mate)

    def vv(j):
        return rc(vp, vbuf.at[y * 4 + z], s_v.at[j], r_v.at[j], chip(j)[2])

    def ww(j):
        return rc(tot, wbuf.at[ci], s_w.at[j], r_w.at[j], fam(j)[1])

    vcopy.start()
    for i in range(NCH):
        cc(i).start()
    for j in range(1, 8):
        ff(j).start()
    vcopy.wait_recv()
    vp[...] = vin[...] + vc[...]
    vbuf[y * 4 + z] = vp[...]
    for j in range(1, 16):
        vv(j).start()
    for i in range(NCH):
        cc(i).wait_recv()
        cbuf[i] = cbuf[i] + lg[pl.ds(mine, 32), i * CW:(i + 1) * CW]
        for j in range(1, 16):
            rs(i, j).start()
    for j in range(1, 16):
        vv(j).wait_recv()
    t = vbuf[0]
    for j in range(1, 16):
        t = t + vbuf[j]
    tot[...] = t
    wbuf[ci] = t
    for j in range(1, 8):
        ww(j).start()
    for i in range(NCH):
        a = cbuf[i, pl.ds(pl.multiple_of(y * 8, 8), 8), pl.ds(pl.multiple_of(z * Q, Q), Q)]
        for j in range(1, 16):
            rs(i, j).wait_recv()
            a = a + rbuf[i, j]
        out[pl.ds(pl.multiple_of(mine + y * 8, 8), 8), pl.ds(pl.multiple_of(i * CW + z * Q, Q), Q)] = a * scale_l
        for j in range(1, 16):
            ag(i, j).start()
    a = fp[pl.ds(pl.multiple_of(ci * 8, 8), 8)]
    for j in range(1, 8):
        ff(j).wait_recv()
        a = a + fbuf[j]
    a = a * scale_f
    for t in range(8):
        fo_ref[t] = a[:, t * 128:(t + 1) * 128]
    for i in range(NCH):
        for j in range(1, 16):
            ag(i, j).wait_recv()
        dd(i).start()
    for j in range(1, 8):
        ww(j).wait_recv()
    t = wbuf[0]
    for j in range(1, 8):
        t = t + wbuf[j]
    vo_ref[0, 0] = jnp.sum(t) * scale_v
    outs = []
    for i in range(NCH):
        dd(i).wait_recv()
        c = pltpu.make_async_copy(out.at[:, pl.ds(i * CW, CW)], lo_ref.at[:, pl.ds(i * CW, CW)], lsem.at[i])
        c.start()
        outs.append(c)
    vcopy.wait_send()
    for j in range(1, 16):
        vv(j).wait_send()
    for j in range(1, 8):
        ff(j).wait_send()
        ww(j).wait_send()
    for i in range(NCH):
        cc(i).wait_send()
        dd(i).wait_send()
        for j in range(1, 16):
            rs(i, j).wait_send()
            ag(i, j).wait_send()
    for c in outs:
        c.wait()


def total_sums(lg, fp, v, scale_l, scale_f, scale_v):
    NCH = 2
    CW = 4096 // NCH
    D = pltpu.SemaphoreType.DMA
    vm = pl.BlockSpec(memory_space=V)
    return pl.pallas_call(
        functools.partial(sums, NCH, scale_l, scale_f, scale_v),
        in_specs=[vm, vm, vm],
        out_specs=[pl.BlockSpec(memory_space=pl.ANY), vm, pl.BlockSpec(memory_space=pltpu.SMEM)],
        out_shape=[jax.ShapeDtypeStruct((64, 4096), F32), jax.ShapeDtypeStruct((8, 8, 128), F32), jax.ShapeDtypeStruct((1, 1), F32)],
        scratch_shapes=[V((NCH, 32, CW), F32), V((NCH, 16, 8, CW // 4), F32), V((64, 4096), F32), V((8, 8, 1024), F32),
                        V((8, 128), F32), V((16, 8, 128), F32), V((8, 128), F32), V((8, 8, 128), F32), V((8, 128), F32),
                        D((NCH,)), D((NCH,)), D((NCH, 16)), D((NCH, 16)), D((NCH, 16)), D((NCH, 16)), D((NCH,)), D((NCH,)),
                        D((8,)), D((8,)), D((16,)), D((16,)), D((8,)), D((8,)), D((NCH,))],
        compiler_params=pltpu.CompilerParams(collective_id=0, has_side_effects=True, vmem_limit_bytes=32 << 20),
    )(lg, fp, v)


def per_device(exposures, defaults, base_rate, loadings, factors, weights):
    paths = lax.axis_size("path") * factors.shape[2]
    cptys = lax.axis_size("cpty") * loadings.shape[0]
    lg, fp, v = own_terms(exposures, defaults, base_rate[None, :], loadings.T, factors, weights)
    lo, fo, vo = total_sums(lg, fp, v, 1.0 / paths, factors.shape[1] / cptys, -1.0 / (math.log(2.0) * cptys * paths))
    return vo[0, 0], lo.T, fo


def solution(mesh):
    in_specs = (P("cpty", None, "path"), P("cpty", "path"), P("cpty"), P("cpty", None), P(None, None, "path"), P())
    out_specs = (P(), P("cpty", None), P(None, "cpty", "path"))
    return jax.shard_map(per_device, mesh=mesh, in_specs=in_specs, out_specs=out_specs, check_vma=False)
```

time: 380 us -> 73.5 us (0.19)
  waiting for transfers between devices: 197 us -> 0 us
  blocking collectives: 82.7 us -> 0 us
  Pallas kernels: 0 us -> 64.3 us
  other arithmetic: 48.2 us -> 0 us
  matrix products: 18.2 us -> 0 us
  between operations: 17.3 us -> 2.48 us
  local copies, waits for them, and re-layouts: 15.4 us -> 6.49 us
    psum x1 -> x0, waiting for transfers between devices: 197 us -> none  [per_device(): loading_grad = lax.psum(loads_part, 'path') / paths]
    psum x1 -> x0, blocking collectives: 82.7 us -> none  [per_device(): value = lax.psum(local_total, ('cpty', 'path')) / (cptys * paths)]
    pallas_call x0 -> x2, Pallas kernels: none -> 64.3 us  [the longest x1 48.3 us: total_sums(): pl.pallas_call(functools.partial(sums, NCH, scale_l, scale_f, scale_v), i...]
    another operation x2 -> x0, other arithmetic: 32.8 us -> none  [the longest x1 20 us: per_device(): hazard = dt_step * jnp.cumsum(rate, axis=1)]
    dot_general x3 -> x0, matrix products: 18.2 us -> none  [the longest x1 8.99 us: per_device(): jnp.einsum('cf,tfp->ctp', loadings, factors, preferred_element_type=jnp.f...]
    convert_element_type x1 -> x0, other arithmetic: 11.8 us -> none  [per_device(): grad_x = (rate * grad_rate).astype(jnp.bfloat16)]
    rev x1 -> x0, local copies, waits for them, and re-layouts: 11.2 us -> none  [per_device(): jnp.flip(weighted, 1)]
  transfers between devices with their start and end apart: 2 -> 0, of which waited for: 1 -> 0; matrix products, arithmetic and copies ran while one was open for 2% -> 0% of each run, Pallas kernels for 0% -> 0%
where the time goes in v1:
time: 73.5 us; the launch traced here: 73.3 us
  Pallas kernels  64.3 us (87%)
  local copies, waits for them, and re-layouts  6.49 us (9%)
  between operations  2.48 us (3%)
    pallas_call x1, Pallas kernels, total_sums(): pl.pallas_call(functools.partial(sums, NCH, scale_l, scale_f, scale_v), i...  48.3 us
    pallas_call x1, Pallas kernels, own_terms(): pl.pallas_call(functools.partial(terms, R, RB, NDMA), in_specs=[A, A, A,...  16 us
    unnamed x12, local copies, waits for them, and re-layouts  6.49 us

profile of v1, /device:TPU:1, one launch (start us, length us, event | category | flops | bytes accessed | tf_op | source)
XLA Modules:
  0.0 73.3 jit_solution(4991679094212027038)
XLA Ops:
  0.6 0.0 copy-start
  0.6 1.6 %copy-done = s32[4096,128]{1,0:T(8,128)S(1)} copy-done((s32[4096,128]{1,0:T(8,128)S(1)}, s32[4096,128]{1,0:T(8,128)}, u32[]{:S(2)}) %copy-start) | copy-done | bytes 2097176
  2.2 0.0 copy-start.1
  2.2 1.0 %copy-done.1 = bf16[4096,64]{0,1:T(8,128)(2,1)S(1)} copy-done((bf16[4096,64]{0,1:T(8,128)(2,1)S(1)}, bf16[4096,64]{0,1:T(8,128)(2,1)}, u32[]{:S(2)}) %copy-start.1) | copy-done | bytes 524312
  3.3 0.0 copy-start.2
  3.3 0.9 %copy-done.2 = bf16[8,64,128]{2,1,0:T(8,128)(2,1)S(1)} copy-done((bf16[8,64,128]{2,1,0:T(8,128)(2,1)S(1)}, bf16[8,64,128]{2,1,0:T(8,128)(2,1)}, u32[]{:S(2)}) %copy-start.2) | copy-done | bytes 131096
  4.2 0.0 copy-start.3
  4.2 0.7 copy-done.3
  4.9 0.0 copy-start.4
  4.9 0.7 copy-done.4
  5.5 16.0 %shard_map.85 = (f32[64,4096]{1,0:T(8,128)S(1)}, f32[64,1024]{1,0:T(8,128)S(1)}, f32[8,128]{1,0:T(8,128)S(1)}) custom-call(bf16[4096,8,128]{2,1,0:T(8,128)(2,1)} %e_hbm.1, s32[4096,128]{1,0:T(8,128)S(1)} %copy-done, f32[1,4096]{1,0:T(1,128)S(1)} %bitcast.6, bf16[64,4096]{1,0:T(8,128)(2,1)S(1)} %bitcast.5, bf16[8,64,128]{2,1,0:T(8,128)(2,1)S(1)} %copy-done.2, ...), custom_call_target="tpu_custom_call" | custom-call | tf_op jit(solution)/shard_map/pallas_call | solution.py:127
  21.5 48.3 %shard_map.86 = (f32[64,4096]{1,0:T(8,128)S(1)}, f32[8,8,128]{2,1,0:T(8,128)S(1)}, f32[1,1]{1,0:T(1,128)}) custom-call(f32[64,4096]{1,0:T(8,128)S(1)} %get-tuple-element.9.lg, f32[64,1024]{1,0:T(8,128)S(1)} %get-tuple-element.10.fp, f32[8,128]{1,0:T(8,128)S(1)} %get-tuple-element.11.vin), custom_call_target="tpu_custom_call" | custom-call | tf_op jit(solution)/shard_map/pallas_call | solution.py:271
  70.5 1.0 %copy.13 = f32[4096,64]{0,1:T(8,128)} copy(f32[4096,64]{0,1:T(8,128)S(1)} %bitcast.4) | data formatting | bytes 2097152
  71.5 0.6 copy.14
Async XLA Ops:
  0.6 1.6 %copy-start = (s32[4096,128]{1,0:T(8,128)S(1)}, s32[4096,128]{1,0:T(8,128)}, u32[]{:S(2)}) copy-start(s32[4096,128]{1,0:T(8,128)} %d_hbm.1) | copy-start | bytes 6291460
  2.2 1.0 %copy-start.1 = (bf16[4096,64]{0,1:T(8,128)(2,1)S(1)}, bf16[4096,64]{0,1:T(8,128)(2,1)}, u32[]{:S(2)}) copy-start(bf16[4096,64]{0,1:T(8,128)(2,1)} %param.9) | copy-start | bytes 1572868
  3.3 0.9 %copy-start.2 = (bf16[8,64,128]{2,1,0:T(8,128)(2,1)S(1)}, bf16[8,64,128]{2,1,0:T(8,128)(2,1)}, u32[]{:S(2)}) copy-start(bf16[8,64,128]{2,1,0:T(8,128)(2,1)} %f_hbm.1) | copy-start | bytes 393220
  4.2 0.7 copy-start.3
  4.9 0.7 copy-start.4

commit v2 on v0

v2 whole, which is shorter than its diff:
```python
import functools
import math

import jax
import jax.numpy as jnp
from jax import lax
from jax.experimental import pallas as pl
from jax.experimental.pallas import tpu as pltpu
from jax.sharding import PartitionSpec as P

LOG2E = 1.4426950408889634
F32, BF = jnp.float32, jnp.bfloat16
MESH = pl.DeviceIdType.MESH
V = pltpu.VMEM


def split3(v):
    h = v.astype(BF)
    r = v - h.astype(F32)
    m = r.astype(BF)
    return h, m, (r - m.astype(F32)).astype(BF)


CT = 4096
R, RB = 256, 32
NB = CT // R
NDMA = 8
CH = CT // NDMA
CW = 1024
NCH = CT // CW
Q = CW // 4
DEF = 4


def kernel(scale_l, scale_f, scale_v, e_hbm, d_hbm, b_hbm, lt_hbm, f_hbm, w_ref, lo_ref, fo_ref, vo_ref,
           e, d, bv, lt, f, f3, f2, ya, yb, ga, gb, gd, fp, lg, v,
           cbuf, ybuf, ysum, zbuf, rbuf, out, fbuf, vc, vp, vbuf, tot, wbuf,
           dsem, ssem, s_c, r_c, s_y, r_y, s_z, r_z, s_az, r_az, s_ay, r_ay, s_d, r_d, s_r, r_r, s_a, r_a,
           s_f, r_f, s_v, r_v, s_w, r_w):
    ci, pi = lax.axis_index("cpty"), lax.axis_index("path")
    y, z, k = pi // 8, (pi // 2) % 4, pi % 2
    mate = (ci, pi - k + (1 - k))

    def chip(j):
        yy, zz = (y + j // 4) % 4, (z + j % 4) % 4
        return yy, zz, (ci, yy * 8 + zz * 2 + k)

    def fam(j):
        cc_ = (ci + j) % 8
        return cc_, (cc_, pi)

    barrier = pltpu.get_barrier_semaphore()
    for dev in [mate] + [chip(j)[2] for j in range(1, 16)] + [fam(j)[1] for j in range(1, 8)]:
        pl.semaphore_signal(barrier, inc=1, device_id=dev, device_id_type=MESH)

    small = [pltpu.make_async_copy(f_hbm, f, ssem.at[0]), pltpu.make_async_copy(lt_hbm, lt, ssem.at[1]),
             pltpu.make_async_copy(b_hbm, bv, ssem.at[2])]
    for c in small:
        c.start()

    def piece(i):
        s = pl.ds(i * CH, CH)
        return (pltpu.make_async_copy(e_hbm.at[s], e.at[s], dsem.at[0, i]),
                pltpu.make_async_copy(d_hbm.at[s], d.at[s], dsem.at[1, i]))

    for i in range(NDMA):
        for c in piece(i):
            c.start()
    for c in small:
        c.wait()
    f3[...] = jnp.zeros_like(f3)
    for t in range(8):
        h, m, l = split3(f[t].astype(F32) * LOG2E)
        sl = slice(t * 128, (t + 1) * 128)
        f3[0:64, sl] = h
        f3[128:192, sl] = m
        f3[192:256, sl] = l
        f2[:, sl] = f[t]
    row = lax.broadcasted_iota(jnp.int32, (16, 1024), 0)
    f3[64:80, :] = jnp.where(row < 3, 1.0, 0.0).astype(BF)
    fp[...] = jnp.zeros_like(fp)
    v[...] = jnp.zeros_like(v)
    gb[...] = jnp.zeros_like(gb)
    wneg = [-math.log(2.0) * w_ref[t] for t in range(8)]

    def ydot(j, yy):
        cs = pl.ds(pl.multiple_of(j * R, R), R)
        l = lt[:, cs]
        h, m, lo = split3(jnp.log2(bv[:, cs] * (0.5 * LOG2E)))
        row = lax.broadcasted_iota(jnp.int32, (16, R), 0)
        extra = jnp.where(row == 0, h.astype(F32), jnp.where(row == 1, m.astype(F32), jnp.where(row == 2, lo.astype(F32), 0.0))).astype(BF)
        l3 = jnp.concatenate([l, extra, jnp.zeros((48, R), BF), l, l], axis=0)
        yy[...] = lax.dot_general(l3, f3[...], (((0,), (0,)), ((), ())), preferred_element_type=F32)

    def elem(j, yy, gx):
        acc = None
        for q in range(R // RB):
            r = pl.multiple_of(j * R + q * RB, RB)
            rl = slice(q * RB, (q + 1) * RB)
            dd_ = d[pl.ds(r, RB), :]
            es = jnp.swapaxes(e[pl.ds(r, RB)], 0, 1).astype(F32)
            rates, wt, hz = [], [], None
            for t in range(8):
                rt = jnp.exp2(yy[rl, t * 128:(t + 1) * 128])
                hz = -rt if t == 0 else hz - rt
                s = jnp.exp2(hz)
                a = jnp.where(t < dd_, es[t], 0.0) * wneg[t]
                rates.append(rt)
                wt.append(a * s)
            g = None
            for t in range(7, -1, -1):
                g = wt[t] if g is None else g + wt[t]
                gx[rl, t * 128:(t + 1) * 128] = (rates[t] * g).astype(BF)
            for n in range(RB // 8):
                part = g[n * 8:(n + 1) * 8]
                acc = part if acc is None else acc + part
        v[...] += acc

    def ddot(j, gx):
        cs = pl.ds(pl.multiple_of(j * R, R), R)
        lg[:, cs] = lax.dot_general(f2[...], gx[...], (((1,), (1,)), ((), ())), preferred_element_type=F32)

    def edot(j, gx):
        cs = pl.ds(pl.multiple_of(j * R, R), R)
        fp[...] += lax.dot_general(lt[:, cs], gx[...], (((1,), (0,)), ((), ())), preferred_element_type=F32)

    def rc(src, dst, ss, rs_, dev):
        return pltpu.make_async_remote_copy(src, dst, ss, rs_, device_id=dev, device_id_type=MESH)

    mine = pl.multiple_of(k * 32, 32)
    other = pl.multiple_of(32 - k * 32, 32)
    rows = pl.ds(pl.multiple_of(mine + y * 8, 8), 8)

    def ycopy(i, j):
        yy, _, dev = chip(4 * j)
        return rc(cbuf.at[i, pl.ds(pl.multiple_of(yy * 8, 8), 8)], ybuf.at[i, j], s_y.at[i, j], r_y.at[i, j], dev)

    def zcopy(i, j):
        _, zz, dev = chip(j)
        return rc(ysum.at[i, :, pl.ds(pl.multiple_of(zz * Q, Q), Q)], zbuf.at[i, j], s_z.at[i, j], r_z.at[i, j], dev)

    def azcopy(i, j):
        p = out.at[rows, pl.ds(pl.multiple_of(i * CW + z * Q, Q), Q)]
        return rc(p, p, s_az.at[i, j], r_az.at[i, j], chip(j)[2])

    def aycopy(i, j):
        p = out.at[rows, pl.ds(i * CW, CW)]
        return rc(p, p, s_ay.at[i, j], r_ay.at[i, j], chip(4 * j)[2])

    def ccopy(i):
        return rc(lg.at[pl.ds(other, 32), pl.ds(i * CW, CW)], cbuf.at[i], s_c.at[i], r_c.at[i], mate)

    def dcopy(i):
        half = out.at[pl.ds(mine, 32), pl.ds(i * CW, CW)]
        return rc(half, half, s_d.at[i], r_d.at[i], mate)

    def rcopy(j):
        yy, zz, dev = chip(j)
        return rc(cbuf.at[NCH - 1, pl.ds(pl.multiple_of(yy * 8, 8), 8), pl.ds(pl.multiple_of(zz * Q, Q), Q)], rbuf.at[j],
                  s_r.at[j], r_r.at[j], dev)

    def acopy(j):
        p = out.at[rows, pl.ds(pl.multiple_of((NCH - 1) * CW + z * Q, Q), Q)]
        return rc(p, p, s_a.at[j], r_a.at[j], chip(j)[2])

    def fcopy(j):
        cc_, dev = fam(j)
        return rc(fp.at[pl.ds(pl.multiple_of(cc_ * 8, 8), 8)], fbuf.at[j], s_f.at[j], r_f.at[j], dev)

    vcopy = rc(v, vc, s_v.at[0], r_v.at[0], mate)

    def vcopies(j):
        return rc(vp, vbuf.at[y * 4 + z], s_v.at[j], r_v.at[j], chip(j)[2])

    def wcopies(j):
        return rc(tot, wbuf.at[ci], s_w.at[j], r_w.at[j], fam(j)[1])

    def core_out(i):
        ccopy(i).start()

    def core_in(i):
        ccopy(i).wait_recv()
        cbuf[i] = cbuf[i] + lg[pl.ds(mine, 32), i * CW:(i + 1) * CW]

    def y_out(i):
        core_in(i)
        for j in (2, 1, 3):
            ycopy(i, j).start()

    def z_out(i):
        a = cbuf[i, pl.ds(pl.multiple_of(y * 8, 8), 8)]
        for j in range(1, 4):
            ycopy(i, j).wait_recv()
            a = a + ybuf[i, j]
        ysum[i] = a
        for j in range(1, 4):
            zcopy(i, j).start()

    def az_out(i):
        a = ysum[i, :, pl.ds(pl.multiple_of(z * Q, Q), Q)]
        for j in range(1, 4):
            zcopy(i, j).wait_recv()
            a = a + zbuf[i, j]
        out[rows, pl.ds(pl.multiple_of(i * CW + z * Q, Q), Q)] = a * scale_l
        for j in range(1, 4):
            azcopy(i, j).start()

    def ay_out(i):
        for j in range(1, 4):
            azcopy(i, j).wait_recv()
        for j in (2, 1, 3):
            aycopy(i, j).start()

    def d_out(i):
        for j in range(1, 4):
            aycopy(i, j).wait_recv()
        dcopy(i).start()

    steps = [core_out, y_out, z_out, az_out, ay_out, d_out]
    at = {2: [(core_out, 0)], 3: [(y_out, 0)], 4: [(core_out, 1)], 5: [(z_out, 0), (y_out, 1)], 6: [(core_out, 2)],
          7: [(az_out, 0), (z_out, 1), (y_out, 2)]}

    piece_per = CH // (2 * R)
    for c in piece(0):
        c.wait()
    ydot(0, ya)

    def body(n, _):
        if piece_per > 1:
            when = (n % piece_per == 0) & (n > 0)
        else:
            when = n > 0

        @pl.when(when)
        def _():
            for c in piece(n // piece_per):
                c.wait()

        j = 2 * n
        ydot(j + 1, yb)
        elem(j, ya, ga)
        ddot(jnp.maximum(j - 1, 0), gb)
        edot(jnp.maximum(j - 1, 0), gb)

        @pl.when(n == 2)
        def _():
            pl.semaphore_wait(barrier, 23)

        for when_, todo in at.items():
            @pl.when(n == when_)
            def _():
                for step, i in todo:
                    step(i)

        ydot(jnp.minimum(j + 2, NB - 1), ya)
        elem(j + 1, yb, gb)
        ddot(j, ga)
        edot(j, ga)
        return 0

    lax.fori_loop(0, NB // 2, body, 0)
    vcopy.start()
    ddot(NB - 1, gb)
    core_out(3)
    vcopy.wait_recv()
    vp[...] = v[...] + vc[...]
    vbuf[y * 4 + z] = vp[...]
    core_in(3)
    for j in range(15, 0, -1):
        rcopy(j).start()
    for j in range(15, 0, -1):
        vcopies(j).start()
    edot(NB - 1, gb)
    for j in range(7, 0, -1):
        fcopy(j).start()
    ay_out(0)
    az_out(1)
    z_out(2)
    a = cbuf[NCH - 1, pl.ds(pl.multiple_of(y * 8, 8), 8), pl.ds(pl.multiple_of(z * Q, Q), Q)]
    for j in range(1, 16):
        rcopy(j).wait_recv()
        a = a + rbuf[j]
    out[rows, pl.ds(pl.multiple_of((NCH - 1) * CW + z * Q, Q), Q)] = a * scale_l
    for j in range(15, 0, -1):
        acopy(j).start()
    for j in range(1, 16):
        vcopies(j).wait_recv()
    t = vbuf[0]
    for j in range(1, 16):
        t = t + vbuf[j]
    tot[...] = t
    wbuf[ci] = t
    for j in range(7, 0, -1):
        wcopies(j).start()
    d_out(0)
    ay_out(1)
    az_out(2)
    d_out(1)
    ay_out(2)
    a = fp[pl.ds(pl.multiple_of(ci * 8, 8), 8)]
    for j in range(1, 8):
        fcopy(j).wait_recv()
        a = a + fbuf[j]
    a = a * scale_f
    for t in range(8):
        fo_ref[t] = a[:, t * 128:(t + 1) * 128]
    d_out(2)
    for j in range(1, 16):
        acopy(j).wait_recv()
    dcopy(3).start()
    for j in range(1, 8):
        wcopies(j).wait_recv()
    t = wbuf[0]
    for j in range(1, 8):
        t = t + wbuf[j]
    vo_ref[0, 0] = jnp.sum(t) * scale_v
    outs = []
    for i in range(NCH):
        dcopy(i).wait_recv()
        c = pltpu.make_async_copy(out.at[:, pl.ds(i * CW, CW)], lo_ref.at[:, pl.ds(i * CW, CW)], ssem.at[i])
        c.start()
        outs.append(c)
    vcopy.wait_send()
    for j in range(1, 16):
        vcopies(j).wait_send()
        rcopy(j).wait_send()
        acopy(j).wait_send()
    for j in range(1, 8):
        fcopy(j).wait_send()
        wcopies(j).wait_send()
    for i in range(NCH):
        ccopy(i).wait_send()
        dcopy(i).wait_send()
    for i in range(NCH - 1):
        for j in range(1, 4):
            ycopy(i, j).wait_send()
            zcopy(i, j).wait_send()
            azcopy(i, j).wait_send()
            aycopy(i, j).wait_send()
    for c in outs:
        c.wait()


def per_device(exposures, defaults, base_rate, loadings, factors, weights):
    paths = lax.axis_size("path") * factors.shape[2]
    cptys = lax.axis_size("cpty") * loadings.shape[0]
    scales = 1.0 / paths, factors.shape[1] / cptys, -1.0 / (math.log(2.0) * cptys * paths)
    A = pl.BlockSpec(memory_space=pl.ANY)
    D = pltpu.SemaphoreType.DMA
    lo, fo, vo = pl.pallas_call(
        functools.partial(kernel, *scales),
        in_specs=[A, A, A, A, A, pl.BlockSpec(memory_space=pltpu.SMEM)],
        out_specs=[A, pl.BlockSpec(memory_space=V), pl.BlockSpec(memory_space=pltpu.SMEM)],
        out_shape=[jax.ShapeDtypeStruct((64, CT), F32), jax.ShapeDtypeStruct((8, 8, 128), F32), jax.ShapeDtypeStruct((1, 1), F32)],
        scratch_shapes=[
            V((CT, 8, 128), BF), V((CT, 128), jnp.int32), V((1, CT), F32), V((64, CT), BF), V((8, 64, 128), BF),
            V((256, 1024), BF), V((64, 1024), BF), V((R, 1024), F32), V((R, 1024), F32), V((R, 1024), BF), V((R, 1024), BF), V((R, 1024), BF),
            V((64, 1024), F32), V((64, CT), F32), V((8, 128), F32),
            V((NCH, 32, CW), F32), V((NCH, 4, 8, CW), F32), V((NCH, 8, CW), F32), V((NCH, 4, 8, Q), F32), V((16, 8, Q), F32), V((64, CT), F32),
            V((8, 8, 1024), F32), V((8, 128), F32), V((8, 128), F32), V((16, 8, 128), F32), V((8, 128), F32), V((8, 8, 128), F32),
            D((2, NDMA)), D((4,)), D((NCH,)), D((NCH,)), D((NCH, 4)), D((NCH, 4)), D((NCH, 4)), D((NCH, 4)), D((NCH, 4)), D((NCH, 4)),
            D((NCH, 4)), D((NCH, 4)), D((NCH,)), D((NCH,)), D((16,)), D((16,)), D((16,)), D((16,)),
            D((8,)), D((8,)), D((16,)), D((16,)), D((8,)), D((8,))],
        compiler_params=pltpu.CompilerParams(collective_id=0, has_side_effects=True, vmem_limit_bytes=60 << 20),
        name="adjoint",
    )(exposures, defaults, base_rate[None, :], loadings.T, factors, weights)
    return vo[0, 0], lo.T, fo


def solution(mesh):
    in_specs = (P("cpty", None, "path"), P("cpty", "path"), P("cpty"), P("cpty", None), P(None, None, "path"), P())
    out_specs = (P(), P("cpty", None), P(None, "cpty", "path"))
    return jax.shard_map(per_device, mesh=mesh, in_specs=in_specs, out_specs=out_specs, check_vma=False)
```

time: 380 us -> 61.7 us (0.16)
  waiting for transfers between devices: 197 us -> 0 us
  blocking collectives: 82.7 us -> 0 us
  Pallas kernels: 0 us -> 55.4 us
  other arithmetic: 48.2 us -> 0 us
  matrix products: 18.2 us -> 0 us
  between operations: 17.3 us -> 2.4 us
  local copies, waits for them, and re-layouts: 15.4 us -> 3.64 us
    psum x1 -> x0, waiting for transfers between devices: 197 us -> none  [per_device(): loading_grad = lax.psum(loads_part, 'path') / paths]
    psum x1 -> x0, blocking collectives: 82.7 us -> none  [per_device(): value = lax.psum(local_total, ('cpty', 'path')) / (cptys * paths)]
    pallas_call x0 -> x1, Pallas kernels: none -> 55.4 us  [per_device(): pl.pallas_call(functools.partial(kernel, *scales), in_specs=[A, A, A, A,...]
    another operation x2 -> x0, other arithmetic: 32.8 us -> none  [the longest x1 20 us: per_device(): hazard = dt_step * jnp.cumsum(rate, axis=1)]
    dot_general x3 -> x0, matrix products: 18.2 us -> none  [the longest x1 8.99 us: per_device(): jnp.einsum('cf,tfp->ctp', loadings, factors, preferred_element_type=jnp.f...]
    convert_element_type x1 -> x0, other arithmetic: 11.8 us -> none  [per_device(): grad_x = (rate * grad_rate).astype(jnp.bfloat16)]
    rev x1 -> x0, local copies, waits for them, and re-layouts: 11.2 us -> none  [per_device(): jnp.flip(weighted, 1)]
  transfers between devices with their start and end apart: 2 -> 0, of which waited for: 1 -> 0; matrix products, arithmetic and copies ran while one was open for 2% -> 0% of each run, Pallas kernels for 0% -> 0%
where the time goes in v2:
time: 61.7 us; the launch traced here: 61.5 us
  Pallas kernels  55.4 us (90%)
  local copies, waits for them, and re-layouts  3.64 us (6%)
  between operations  2.4 us (4%)
    pallas_call x1, Pallas kernels, per_device(): pl.pallas_call(functools.partial(kernel, *scales), in_specs=[A, A, A, A,...  55.4 us
    unnamed x2, local copies, waits for them, and re-layouts  3.64 us

profile of v2, /device:TPU:1, one launch (start us, length us, event | category | flops | bytes accessed | tf_op | source)
XLA Modules:
  0.0 61.5 jit_solution(17524996625112767803)
XLA Ops:
  0.6 55.4 %adjoint.1 = (f32[64,4096]{1,0:T(8,128)}, f32[8,8,128]{2,1,0:T(8,128)}, f32[1,1]{1,0:T(1,128)}) custom-call(bf16[4096,8,128]{2,1,0:T(8,128)(2,1)} %e_hbm.1, s32[4096,128]{1,0:T(8,128)} %d_hbm.1, f32[1,4096]{1,0:T(1,128)} %bitcast.6, bf16[64,4096]{1,0:T(8,128)(2,1)} %bitcast.5, bf16[8,64,128]{2,1,0:T(8,128)(2,1)} %f_hbm.1, f32[8]{0:T(128)} %w_ref.1), custom_call_target="tpu_custom_call" | custom-call | tf_op jit(solution)/shard_map/adjoint/pallas_call | solution.py:350
  56.7 2.3 %copy.13 = f32[4096,64]{0,1:T(8,128)} copy(f32[4096,64]{0,1:T(8,128)} %bitcast.4) | data formatting | bytes 2097152
  59.0 1.4 %copy.14 = f32[8,8,128]{2,1,0:T(8,128)} copy(f32[8,8,128]{2,1,0:T(8,128)} %get-tuple-element.14) | data formatting | bytes 65536

commit v3 on v0

v3 whole, which is shorter than its diff:
```python
import functools
import math

import jax
import jax.numpy as jnp
from jax import lax
from jax.experimental import pallas as pl
from jax.experimental.pallas import tpu as pltpu
from jax.sharding import PartitionSpec as P

LOG2E = 1.4426950408889634
F32, BF = jnp.float32, jnp.bfloat16
MESH = pl.DeviceIdType.MESH
V = pltpu.VMEM


def split3(v):
    h = v.astype(BF)
    r = v - h.astype(F32)
    m = r.astype(BF)
    return h, m, (r - m.astype(F32)).astype(BF)


CT = 4096
R, RB = 256, 16
NB = CT // R
CH = 2 * R
AHEAD = 4
ENDS = (1280, 2304, 3328, 4096)


def kernel(scale_l, scale_f, scale_v, e_hbm, d_hbm, b_hbm, lt_hbm, f_hbm, w_ref, lo_ref, fo_ref, vo_ref,
           e, d, bv, lt, f, f3, f2, ya, yb, et, gall, fp, lg, v, cbuf, ybuf, zbuf, fx, fz, vc, vy, vx, vz,
           dsem, ssem, s_c, r_c, s_y, r_y, s_z, r_z, s_a, r_a, s_d, r_d, s_f, r_f, s_v, r_v):
    ci, pi = lax.axis_index("cpty"), lax.axis_index("path")
    zh, x = ci // 4, ci % 4
    y, z, k = pi // 8, (pi // 2) % 4, pi % 2
    z8 = zh * 4 + z
    mate = (ci, pi - k + (1 - k))

    def ypeer(j):
        yy = (y + j) % 4
        return yy, (ci, yy * 8 + z * 2 + k)

    def zpeer(j):
        return (ci, y * 8 + ((z + j) % 4) * 2 + k)

    def xpeer(j):
        xx = (x + j) % 4
        return xx, (zh * 4 + xx, pi)

    def ringpeer(j):
        zz = (z8 + j) % 8
        return ((zz // 4) * 4 + x, y * 8 + (zz % 4) * 2 + k)

    zhpeer = ((1 - zh) * 4 + x, pi)

    small = [pltpu.make_async_copy(f_hbm, f, ssem.at[0]), pltpu.make_async_copy(lt_hbm, lt, ssem.at[1]),
             pltpu.make_async_copy(b_hbm, bv, ssem.at[2])]
    for c in small:
        c.start()

    def piece(i):
        s = pl.ds(pl.multiple_of(i * CH, CH), CH)
        return (pltpu.make_async_copy(e_hbm.at[s], e.at[s], dsem.at[0, i]),
                pltpu.make_async_copy(d_hbm.at[s], d.at[s], dsem.at[1, i]))

    for i in range(AHEAD):
        for c in piece(i):
            c.start()
    barrier = pltpu.get_barrier_semaphore()
    peers = [mate] + [ypeer(j)[1] for j in range(1, 4)] + [xpeer(j)[1] for j in range(1, 4)] + [ringpeer(j) for j in range(1, 8)]
    for dev in peers:
        pl.semaphore_signal(barrier, inc=1, device_id=dev, device_id_type=MESH)
    f3[64:128, :] = jnp.zeros((64, 1024), BF)
    row = lax.broadcasted_iota(jnp.int32, (16, 1024), 0)
    f3[64:80, :] = jnp.where(row < 3, 1.0, 0.0).astype(BF)
    v[...] = jnp.zeros_like(v)
    gall[pl.ds(0, R), :] = jnp.zeros((R, 1024), BF)
    for c in small:
        c.wait()
    for t in range(8):
        h, m, l = split3(f[t].astype(F32) * LOG2E)
        sl = slice(t * 128, (t + 1) * 128)
        f3[0:64, sl] = h
        f3[128:192, sl] = m
        f3[192:256, sl] = l
        f2[:, sl] = f[t]
    wneg = [-math.log(2.0) * w_ref[t] for t in range(8)]

    def ydot(j, yy):
        cs = pl.ds(pl.multiple_of(j * R, R), R)
        l = lt[:, cs]
        h, m, lo = split3(jnp.log2(bv[:, cs] * (0.5 * LOG2E)))
        row = lax.broadcasted_iota(jnp.int32, (16, R), 0)
        extra = jnp.where(row == 0, h.astype(F32), jnp.where(row == 1, m.astype(F32), jnp.where(row == 2, lo.astype(F32), 0.0))).astype(BF)
        l3 = jnp.concatenate([l, extra, jnp.zeros((48, R), BF), l, l], axis=0)
        yy[...] = lax.dot_general(l3, f3[...], (((0,), (0,)), ((), ())), preferred_element_type=F32)

    def elem(j, yy):
        acc = None
        for q in range(R // RB):
            r = pl.multiple_of(j * R + q * RB, RB)
            rl = slice(q * RB, (q + 1) * RB)
            dd_ = d[pl.ds(r, RB), :]
            et[q * RB * 8:(q + 1) * RB * 8, :] = e[pl.ds(r, RB)].astype(F32).reshape(RB * 8, 128)
            rates, wt, hz = [], [], None
            for t in range(8):
                rt = jnp.exp2(yy[rl, t * 128:(t + 1) * 128])
                hz = -rt if t == 0 else hz - rt
                s = jnp.exp2(hz)
                a = jnp.where(t < dd_, et[pl.ds(q * RB * 8 + t, RB, stride=8), :], 0.0) * wneg[t]
                rates.append(rt)
                wt.append(a * s)
            g = None
            for t in range(7, -1, -1):
                g = wt[t] if g is None else g + wt[t]
                gall[pl.ds(r, RB), t * 128:(t + 1) * 128] = (rates[t] * g).astype(BF)
            for n in range(RB // 8):
                part = g[n * 8:(n + 1) * 8]
                acc = part if acc is None else acc + part
        v[...] += acc

    def ddot(j):
        cs = pl.ds(pl.multiple_of(j * R, R), R)
        lg[:, cs] = lax.dot_general(f2[...], gall[cs, :], (((1,), (1,)), ((), ())), preferred_element_type=F32)

    def rc(src, dst, ss, rs_, dev):
        return pltpu.make_async_remote_copy(src, dst, ss, rs_, device_id=dev, device_id_type=MESH)

    mine = pl.multiple_of(k * 32, 32)
    other = pl.multiple_of(32 - k * 32, 32)
    rows = pl.ds(pl.multiple_of(mine + y * 8, 8), 8)

    def cols(i):
        lo = 0 if i == 0 else ENDS[i - 1]
        return pl.ds(lo, ENDS[i] - lo)

    def ccopy(i):
        return rc(lg.at[pl.ds(other, 32), cols(i)], cbuf.at[:, cols(i)], s_c.at[i], r_c.at[i], mate)

    def ycopy(i, j):
        yy, dev = ypeer(j)
        return rc(cbuf.at[pl.ds(pl.multiple_of(yy * 8, 8), 8), cols(i)], ybuf.at[j, :, cols(i)], s_y.at[i, j], r_y.at[i, j], dev)

    def zcopy(i, j):
        p = zbuf.at[z, :, cols(i)]
        return rc(p, p, s_z.at[i, j], r_z.at[i, j], zpeer(j))

    def acopy(i, j):
        p = lo_ref.at[rows, cols(i)]
        return rc(p, p, s_a.at[i, j], r_a.at[i, j], ypeer(j)[1])

    def dcopy(i):
        half = lo_ref.at[pl.ds(mine, 32), cols(i)]
        return rc(half, half, s_d.at[i], r_d.at[i], mate)

    def core_out(i):
        ccopy(i).start()

    def y_out(i):
        ccopy(i).wait_recv()
        cbuf[:, cols(i)] = cbuf[:, cols(i)] + lg[pl.ds(mine, 32), cols(i)]
        for j in (2, 1, 3):
            ycopy(i, j).start()

    def z_out(i):
        a = cbuf[pl.ds(pl.multiple_of(y * 8, 8), 8), cols(i)]
        for j in range(1, 4):
            ycopy(i, j).wait_recv()
            a = a + ybuf[j, :, cols(i)]
        zbuf[z, :, cols(i)] = a
        for j in range(1, 4):
            zcopy(i, j).start()

    def a_out(i):
        for j in range(1, 4):
            zcopy(i, j).wait_recv()
        a = (zbuf[0, :, cols(i)] + zbuf[1, :, cols(i)]) + (zbuf[2, :, cols(i)] + zbuf[3, :, cols(i)])
        lo_ref[rows, cols(i)] = a * scale_l
        for j in (2, 1, 3):
            acopy(i, j).start()

    def d_out(i):
        for j in range(1, 4):
            acopy(i, j).wait_recv()
        dcopy(i).start()

    def fcopy(j):
        xx, dev = xpeer(j)
        return rc(fp.at[:, xx], fx.at[j], s_f.at[j], r_f.at[j], dev)

    fzcopy = rc(fz.at[1 - zh], fz.at[2], s_f.at[0], r_f.at[0], zhpeer)
    vcopy = rc(v, vc, s_v.at[0], r_v.at[0], mate)

    def vycopy(j):
        return rc(vy.at[y], vy.at[y], s_v.at[j], r_v.at[j], ypeer(j)[1])

    def vxcopy(j):
        return rc(vx.at[x], vx.at[x], s_v.at[3 + j], r_v.at[3 + j], xpeer(j)[1])

    def vzcopy(j):
        return rc(vz.at[z8], vz.at[z8], s_v.at[6 + j], r_v.at[6 + j], ringpeer(j))

    at = {2: [(core_out, 0)], 3: [(y_out, 0)], 4: [(core_out, 1)], 5: [(y_out, 1)], 6: [(core_out, 2), (z_out, 0)], 7: [(y_out, 2)]}

    ydot(0, ya)

    def body(n, _):
        @pl.when(n < NB // 2 - AHEAD)
        def _():
            for c in piece(n + AHEAD):
                c.start()

        for c in piece(n):
            c.wait()
        j = 2 * n
        ydot(j + 1, yb)
        elem(j, ya)
        ddot(jnp.maximum(j - 1, 0))
        ydot(jnp.minimum(j + 2, NB - 1), ya)
        elem(j + 1, yb)
        ddot(j)

        @pl.when(n == 2)
        def _():
            pl.semaphore_wait(barrier, len(peers))

        for when_, todo in at.items():
            @pl.when(n == when_)
            def _():
                for step, i in todo:
                    step(i)

        return 0

    lax.fori_loop(0, NB // 2, body, 0)
    ddot(NB - 1)
    core_out(3)
    vcopy.start()
    z_out(1)
    y_out(3)
    vcopy.wait_recv()
    vy[y] = v[...] + vc[...]
    for j in (2, 1, 3):
        vycopy(j).start()
    for t in range(0, 8, 2):
        part = lax.dot_general(lt[...], gall[:, t * 128:(t + 2) * 128], (((1,), (0,)), ((), ())), preferred_element_type=F32)
        fp[:, :, :, t * 128:(t + 2) * 128] = part.reshape(2, 4, 8, 256)
    for j in (2, 1, 3):
        fcopy(j).start()
    z_out(2)
    for j in range(1, 4):
        vycopy(j).wait_recv()
    vx[x] = (vy[0] + vy[1]) + (vy[2] + vy[3])
    for j in (2, 1, 3):
        vxcopy(j).start()
    z_out(3)
    a_out(0)
    a_out(1)
    for j in range(1, 4):
        vxcopy(j).wait_recv()
    vz[z8] = (vx[0] + vx[1]) + (vx[2] + vx[3])
    for j in (4, 3, 5, 2, 6, 1, 7):
        vzcopy(j).start()
    a = fp[:, x]
    for j in range(1, 4):
        fcopy(j).wait_recv()
        a = a + fx[j]
    fz[0:2] = a
    fzcopy.start()
    a_out(2)
    d_out(0)
    a_out(3)
    d_out(1)
    for j in range(1, 8):
        vzcopy(j).wait_recv()
    a = ((vz[0] + vz[1]) + (vz[2] + vz[3])) + ((vz[4] + vz[5]) + (vz[6] + vz[7]))
    vo_ref[0, 0] = jnp.sum(a) * scale_v
    fzcopy.wait_recv()
    a = (fz[zh] + fz[2]) * scale_f
    for t in range(8):
        fo_ref[t] = a[:, t * 128:(t + 1) * 128]
    d_out(2)
    d_out(3)
    vcopy.wait_send()
    fzcopy.wait_send()
    for j in range(1, 4):
        vycopy(j).wait_send()
        vxcopy(j).wait_send()
        fcopy(j).wait_send()
    for j in range(1, 8):
        vzcopy(j).wait_send()
    for i in range(4):
        ccopy(i).wait_send()
        for j in range(1, 4):
            ycopy(i, j).wait_send()
            zcopy(i, j).wait_send()
            acopy(i, j).wait_send()
        dcopy(i).wait_recv()
        dcopy(i).wait_send()


def per_device(exposures, defaults, base_rate, loadings, factors, weights):
    paths = lax.axis_size("path") * factors.shape[2]
    cptys = lax.axis_size("cpty") * loadings.shape[0]
    scales = 1.0 / paths, factors.shape[1] / cptys, -1.0 / (math.log(2.0) * cptys * paths)
    A = pl.BlockSpec(memory_space=pl.ANY)
    H = pl.BlockSpec(memory_space=pltpu.HBM)
    S = pl.BlockSpec(memory_space=pltpu.SMEM)
    D = pltpu.SemaphoreType.DMA
    shapes = [jax.ShapeDtypeStruct((64, CT), F32), jax.ShapeDtypeStruct((8, 8, 128), F32), jax.ShapeDtypeStruct((1, 1), F32)]
    lo, fo, vo = pl.pallas_call(
        functools.partial(kernel, *scales),
        in_specs=[H, H, H, H, H, S],
        out_specs=[pl.BlockSpec(memory_space=V), pl.BlockSpec(memory_space=V), S],
        out_shape=shapes,
        scratch_shapes=[
            V((CT, 8, 128), BF), V((CT, 128), jnp.int32), V((1, CT), F32), V((64, CT), BF), V((8, 64, 128), BF),
            V((256, 1024), BF), V((64, 1024), BF), V((R, 1024), F32), V((R, 1024), F32), V((R * 8, 128), F32), V((CT, 1024), BF),
            V((2, 4, 8, 1024), F32), V((64, CT), F32), V((8, 128), F32),
            V((32, CT), F32), V((4, 8, CT), F32), V((4, 8, CT), F32),
            V((4, 2, 8, 1024), F32), V((3, 8, 1024), F32), V((8, 128), F32), V((4, 8, 128), F32), V((4, 8, 128), F32), V((8, 8, 128), F32),
            D((2, NB // 2)), D((4,)), D((4,)), D((4,)), D((4, 4)), D((4, 4)), D((4, 4)), D((4, 4)), D((4, 4)), D((4, 4)), D((4,)), D((4,)),
            D((4,)), D((4,)), D((16,)), D((16,))],
        compiler_params=pltpu.CompilerParams(collective_id=0, has_side_effects=True, vmem_limit_bytes=44 << 20),
        name="adjoint",
    )(*(pltpu.with_memory_space_constraint(a, pltpu.HBM) for a in (exposures, defaults, base_rate[None, :], loadings.T, factors, weights)))
    return vo[0, 0], lo.T, fo


def solution(mesh):
    in_specs = (P("cpty", None, "path"), P("cpty", "path"), P("cpty"), P("cpty", None), P(None, None, "path"), P())
    out_specs = (P(), P("cpty", None), P(None, "cpty", "path"))
    return jax.shard_map(per_device, mesh=mesh, in_specs=in_specs, out_specs=out_specs, check_vma=False)
```

time: 380 us -> 44.7 us (0.12)
  waiting for transfers between devices: 197 us -> 0 us
  blocking collectives: 82.7 us -> 0 us
  other arithmetic: 48.2 us -> 0 us
  Pallas kernels: 0 us -> 40.7 us
  matrix products: 18.2 us -> 0 us
  between operations: 17.3 us -> 2.33 us
  local copies, waits for them, and re-layouts: 15.4 us -> 1.59 us
    psum x1 -> x0, waiting for transfers between devices: 197 us -> none  [per_device(): loading_grad = lax.psum(loads_part, 'path') / paths]
    psum x1 -> x0, blocking collectives: 82.7 us -> none  [per_device(): value = lax.psum(local_total, ('cpty', 'path')) / (cptys * paths)]
    pallas_call x0 -> x1, Pallas kernels: none -> 40.7 us  [per_device(): pl.pallas_call(functools.partial(kernel, *scales), in_specs=[H, H, H, H,...]
    another operation x2 -> x0, other arithmetic: 32.8 us -> none  [the longest x1 20 us: per_device(): hazard = dt_step * jnp.cumsum(rate, axis=1)]
    dot_general x3 -> x0, matrix products: 18.2 us -> none  [the longest x1 8.99 us: per_device(): jnp.einsum('cf,tfp->ctp', loadings, factors, preferred_element_type=jnp.f...]
    convert_element_type x1 -> x0, other arithmetic: 11.8 us -> none  [per_device(): grad_x = (rate * grad_rate).astype(jnp.bfloat16)]
    rev x1 -> x0, local copies, waits for them, and re-layouts: 11.2 us -> none  [per_device(): jnp.flip(weighted, 1)]
  transfers between devices with their start and end apart: 2 -> 0, of which waited for: 1 -> 0; matrix products, arithmetic and copies ran while one was open for 2% -> 0% of each run, Pallas kernels for 0% -> 0%
where the time goes in v3:
time: 44.7 us; the launch traced here: 44.6 us
  Pallas kernels  40.7 us (91%)
  between operations  2.33 us (5%)
  local copies, waits for them, and re-layouts  1.59 us (4%)
    pallas_call x1, Pallas kernels, per_device(): pl.pallas_call(functools.partial(kernel, *scales), in_specs=[H, H, H, H,...  40.7 us
    unnamed x2, local copies, waits for them, and re-layouts  1.59 us

profile of v3, /device:TPU:1, one launch (start us, length us, event | category | flops | bytes accessed | tf_op | source)
XLA Modules:
  0.0 44.6 jit_solution(11306129892631526535)
XLA Ops:
  0.6 40.7 %adjoint.1 = (f32[64,4096]{1,0:T(8,128)S(1)}, f32[8,8,128]{2,1,0:T(8,128)S(1)}, f32[1,1]{1,0:T(1,128)}) custom-call(bf16[4096,8,128]{2,1,0:T(8,128)(2,1)} %e_hbm.1, s32[4096,128]{1,0:T(8,128)} %d_hbm.1, f32[1,4096]{1,0:T(1,128)} %bitcast.6, bf16[64,4096]{1,0:T(8,128)(2,1)} %bitcast.5, bf16[8,64,128]{2,1,0:T(8,128)(2,1)} %f_hbm.1, f32[8]{0:T(128)} %w_ref.1), custom_call_target="tpu_custom_call" | custom-call | tf_op jit(solution)/shard_map/adjoint/pallas_call | solution.py:313
  41.9 1.0 %copy.13 = f32[4096,64]{0,1:T(8,128)} copy(f32[4096,64]{0,1:T(8,128)S(1)} %bitcast.4) | data formatting | bytes 2097152
  42.8 0.6 %copy.14 = f32[8,8,128]{2,1,0:T(8,128)} copy(f32[8,8,128]{2,1,0:T(8,128)S(1)} %get-tuple-element.14) | data formatting | bytes 65536

commit v4 on v3

--- a/solution.py
+++ b/solution.py
@@ -25,7 +25,7 @@
 R, RB = 256, 16
 NB = CT // R
 CH = 2 * R
-AHEAD = 4
+AHEAD = 1
 ENDS = (1280, 2304, 3328, 4096)
 
 
@@ -104,21 +104,24 @@
             rl = slice(q * RB, (q + 1) * RB)
             dd_ = d[pl.ds(r, RB), :]
             et[q * RB * 8:(q + 1) * RB * 8, :] = e[pl.ds(r, RB)].astype(F32).reshape(RB * 8, 128)
-            rates, wt, hz = [], [], None
+            sums = []
+            for o in range(0, RB, 8):
+                rates, wt, hz = [], [], None
+                for t in range(8):
+                    rt = jnp.exp2(yy[q * RB + o:q * RB + o + 8, t * 128:(t + 1) * 128])
+                    hz = -rt if t == 0 else hz - rt
+                    s = jnp.exp2(hz)
+                    a = jnp.where(t < dd_[o:o + 8], et[pl.ds((q * RB + o) * 8 + t, 8, stride=8), :], 0.0) * wneg[t]
+                    rates.append(rt)
+                    wt.append(a * s)
+                g = None
+                for t in range(7, -1, -1):
+                    g = wt[t] if g is None else g + wt[t]
+                    rates[t] = rates[t] * g
+                sums.append(rates)
+                acc = g if acc is None else acc + g
             for t in range(8):
-                rt = jnp.exp2(yy[rl, t * 128:(t + 1) * 128])
-                hz = -rt if t == 0 else hz - rt
-                s = jnp.exp2(hz)
-                a = jnp.where(t < dd_, et[pl.ds(q * RB * 8 + t, RB, stride=8), :], 0.0) * wneg[t]
-                rates.append(rt)
-                wt.append(a * s)
-            g = None
-            for t in range(7, -1, -1):
-                g = wt[t] if g is None else g + wt[t]
-                gall[pl.ds(r, RB), t * 128:(t + 1) * 128] = (rates[t] * g).astype(BF)
-            for n in range(RB // 8):
-                part = g[n * 8:(n + 1) * 8]
-                acc = part if acc is None else acc + part
+                gall[pl.ds(r, RB), t * 128:(t + 1) * 128] = jnp.concatenate([rates[t] for rates in sums], axis=0).astype(BF)
         v[...] += acc
 
     def ddot(j):
@@ -276,7 +279,7 @@
     for j in range(1, 8):
         vzcopy(j).wait_recv()
     a = ((vz[0] + vz[1]) + (vz[2] + vz[3])) + ((vz[4] + vz[5]) + (vz[6] + vz[7]))
-    vo_ref[0, 0] = jnp.sum(a) * scale_v
+    vo_ref[...] = jnp.sum(a, axis=(0, 1), keepdims=True) * scale_v
     fzcopy.wait_recv()
     a = (fz[zh] + fz[2]) * scale_f
     for t in range(8):
@@ -301,6 +304,15 @@
         dcopy(i).wait_send()
 
 
+def finish(lo, fo, vo, lo_ref, fo_ref, vo_ref, sem):
+    copies = [pltpu.make_async_copy(lo.at[pl.ds(8 * i, 8)], lo_ref.at[pl.ds(8 * i, 8)], sem.at[i]) for i in range(8)]
+    copies += [pltpu.make_async_copy(fo, fo_ref, sem.at[8]), pltpu.make_async_copy(vo, vo_ref, sem.at[9])]
+    for c in copies:
+        c.start()
+    for c in copies:
+        c.wait()
+
+
 def per_device(exposures, defaults, base_rate, loadings, factors, weights):
     paths = lax.axis_size("path") * factors.shape[2]
     cptys = lax.axis_size("cpty") * loadings.shape[0]
@@ -313,7 +325,7 @@
     lo, fo, vo = pl.pallas_call(
         functools.partial(kernel, *scales),
         in_specs=[H, H, H, H, H, S],
-        out_specs=[pl.BlockSpec(memory_space=V), pl.BlockSpec(memory_space=V), S],
+        out_specs=[pl.BlockSpec(memory_space=V)] * 3,
         out_shape=shapes,
         scratch_shapes=[
             V((CT, 8, 128), BF), V((CT, 128), jnp.int32), V((1, CT), F32), V((64, CT), BF), V((8, 64, 128), BF),
@@ -326,6 +338,15 @@
         compiler_params=pltpu.CompilerParams(collective_id=0, has_side_effects=True, vmem_limit_bytes=44 << 20),
         name="adjoint",
     )(*(pltpu.with_memory_space_constraint(a, pltpu.HBM) for a in (exposures, defaults, base_rate[None, :], loadings.T, factors, weights)))
+    lo, fo, vo = (pltpu.with_memory_space_constraint(a, pltpu.VMEM) for a in (lo, fo, vo))
+    lo, fo, vo = pl.pallas_call(
+        finish,
+        in_specs=[A, A, A],
+        out_specs=[H, H, H],
+        out_shape=shapes,
+        scratch_shapes=[D((10,))],
+        name="finish",
+    )(lo, fo, vo)
     return vo[0, 0], lo.T, fo
 
 

time: 44.7 us -> 41.7 us (0.933)
  between operations: 2.33 us -> 0.64 us
  local copies, waits for them, and re-layouts: 1.59 us -> 0 us
    pallas_call x0 -> x1, Pallas kernels: none -> 1.68 us  [per_device(): pl.pallas_call(finish, in_specs=[A, A, A], out_specs=[H, H, H], out_shape...]
    unnamed x2 -> x0, local copies, waits for them, and re-layouts: 1.59 us -> none
    pallas_call x1, Pallas kernels: 40.7 us -> 39.2 us  [per_device(): pl.pallas_call(functools.partial(kernel, *scales), in_specs=[H, H, H, H,...]
where the time goes in v4:
time: 41.7 us; the launch traced here: 41.5 us
  Pallas kernels  40.9 us (98%)
  between operations  0.64 us (2%)
    pallas_call x1, Pallas kernels, per_device(): pl.pallas_call(functools.partial(kernel, *scales), in_specs=[H, H, H, H,...  39.2 us
    pallas_call x1, Pallas kernels, per_device(): pl.pallas_call(finish, in_specs=[A, A, A], out_specs=[H, H, H], out_shape...  1.68 us

profile of v4, /device:TPU:1, one launch (start us, length us, event | category | flops | bytes accessed | tf_op | source)
XLA Modules:
  0.0 41.5 jit_solution(13334186664250701249)
XLA Ops:
  0.6 39.2 %adjoint.1 = (f32[64,4096]{1,0:T(8,128)S(1)}, f32[8,8,128]{2,1,0:T(8,128)S(1)}, f32[1,1]{1,0:T(1,128)}) custom-call(bf16[4096,8,128]{2,1,0:T(8,128)(2,1)} %e_hbm.1, s32[4096,128]{1,0:T(8,128)} %d_hbm.1, f32[1,4096]{1,0:T(1,128)} %bitcast.5, bf16[64,4096]{1,0:T(8,128)(2,1)} %bitcast.4, bf16[8,64,128]{2,1,0:T(8,128)(2,1)} %f_hbm.1, f32[8]{0:T(128)} %w_ref.1), custom_call_target="tpu_custom_call" | custom-call | tf_op jit(solution)/shard_map/adjoint/pallas_call | solution.py:325
  39.9 1.7 %finish.1 = (f32[64,4096]{1,0:T(8,128)}, f32[8,8,128]{2,1,0:T(8,128)}, f32[1,1]{1,0:T(1,128)}) custom-call(f32[64,4096]{1,0:T(8,128)S(1)} %get-tuple-element.9.lo, f32[8,8,128]{2,1,0:T(8,128)S(1)} %get-tuple-element.10.fo, f32[1,1]{1,0:T(1,128)} %get-tuple-element.11.vo), custom_call_target="tpu_custom_call" | custom-call | tf_op jit(solution)/shard_map/finish/pallas_call | solution.py:342

commit v5 on v4

--- a/solution.py
+++ b/solution.py
@@ -29,9 +29,9 @@
 ENDS = (1280, 2304, 3328, 4096)
 
 
-def kernel(scale_l, scale_f, scale_v, e_hbm, d_hbm, b_hbm, lt_hbm, f_hbm, w_ref, lo_ref, fo_ref, vo_ref,
+def kernel(scale_l, scale_f, scale_v, e_hbm, d_hbm, b_hbm, lt_hbm, f_hbm, w_hbm, lo_ref, fo_ref, vo_ref,
            e, d, bv, lt, f, f3, f2, ya, yb, et, gall, fp, lg, v, cbuf, ybuf, zbuf, fx, fz, vc, vy, vx, vz,
-           dsem, ssem, s_c, r_c, s_y, r_y, s_z, r_z, s_a, r_a, s_d, r_d, s_f, r_f, s_v, r_v):
+           w_ref, dsem, ssem, s_c, r_c, s_y, r_y, s_z, r_z, s_a, r_a, s_d, r_d, s_f, r_f, s_v, r_v):
     ci, pi = lax.axis_index("cpty"), lax.axis_index("path")
     zh, x = ci // 4, ci % 4
     y, z, k = pi // 8, (pi // 2) % 4, pi % 2
@@ -56,7 +56,7 @@
     zhpeer = ((1 - zh) * 4 + x, pi)
 
     small = [pltpu.make_async_copy(f_hbm, f, ssem.at[0]), pltpu.make_async_copy(lt_hbm, lt, ssem.at[1]),
-             pltpu.make_async_copy(b_hbm, bv, ssem.at[2])]
+             pltpu.make_async_copy(b_hbm, bv, ssem.at[2]), pltpu.make_async_copy(w_hbm, w_ref, ssem.at[3])]
     for c in small:
         c.start()
 
@@ -319,12 +319,11 @@
     scales = 1.0 / paths, factors.shape[1] / cptys, -1.0 / (math.log(2.0) * cptys * paths)
     A = pl.BlockSpec(memory_space=pl.ANY)
     H = pl.BlockSpec(memory_space=pltpu.HBM)
-    S = pl.BlockSpec(memory_space=pltpu.SMEM)
     D = pltpu.SemaphoreType.DMA
     shapes = [jax.ShapeDtypeStruct((64, CT), F32), jax.ShapeDtypeStruct((8, 8, 128), F32), jax.ShapeDtypeStruct((1, 1), F32)]
     lo, fo, vo = pl.pallas_call(
         functools.partial(kernel, *scales),
-        in_specs=[H, H, H, H, H, S],
+        in_specs=[H] * 6,
         out_specs=[pl.BlockSpec(memory_space=V)] * 3,
         out_shape=shapes,
         scratch_shapes=[
@@ -333,7 +332,7 @@
             V((2, 4, 8, 1024), F32), V((64, CT), F32), V((8, 128), F32),
             V((32, CT), F32), V((4, 8, CT), F32), V((4, 8, CT), F32),
             V((4, 2, 8, 1024), F32), V((3, 8, 1024), F32), V((8, 128), F32), V((4, 8, 128), F32), V((4, 8, 128), F32), V((8, 8, 128), F32),
-            D((2, NB // 2)), D((4,)), D((4,)), D((4,)), D((4, 4)), D((4, 4)), D((4, 4)), D((4, 4)), D((4, 4)), D((4, 4)), D((4,)), D((4,)),
+            pltpu.SMEM((8,), F32), D((2, NB // 2)), D((4,)), D((4,)), D((4,)), D((4, 4)), D((4, 4)), D((4, 4)), D((4, 4)), D((4, 4)), D((4, 4)), D((4,)), D((4,)),
             D((4,)), D((4,)), D((16,)), D((16,))],
         compiler_params=pltpu.CompilerParams(collective_id=0, has_side_effects=True, vmem_limit_bytes=44 << 20),
         name="adjoint",

time: 41.7 us -> 40.8 us (0.978)
  Pallas kernels: 40.9 us -> 40.1 us
    pallas_call x1, Pallas kernels: 39.2 us -> 38.4 us  [per_device(): pl.pallas_call(functools.partial(kernel, *scales), in_specs=[H] * 6, out_...]
where the time goes in v5:
time: 40.8 us; the launch traced here: 40.7 us
  Pallas kernels  40.1 us (98%)
  between operations  0.64 us (2%)
    pallas_call x1, Pallas kernels, per_device(): pl.pallas_call(functools.partial(kernel, *scales), in_specs=[H] * 6, out_...  38.4 us
    pallas_call x1, Pallas kernels, per_device(): pl.pallas_call(finish, in_specs=[A, A, A], out_specs=[H, H, H], out_shape...  1.68 us

profile of v5, /device:TPU:1, one launch (start us, length us, event | category | flops | bytes accessed | tf_op | source)
XLA Modules:
  0.0 40.7 jit_solution(16846925934858735084)
XLA Ops:
  0.6 38.4 %adjoint.1 = (f32[64,4096]{1,0:T(8,128)S(1)}, f32[8,8,128]{2,1,0:T(8,128)S(1)}, f32[1,1]{1,0:T(1,128)}) custom-call(bf16[4096,8,128]{2,1,0:T(8,128)(2,1)} %e_hbm.1, s32[4096,128]{1,0:T(8,128)} %d_hbm.1, f32[1,4096]{1,0:T(1,128)} %bitcast.5, bf16[64,4096]{1,0:T(8,128)(2,1)} %bitcast.4, bf16[8,64,128]{2,1,0:T(8,128)(2,1)} %f_hbm.1, f32[8]{0:T(128)} %w_hbm.1), custom_call_target="tpu_custom_call" | custom-call | tf_op jit(solution)/shard_map/adjoint/pallas_call | solution.py:324
  39.0 1.7 %finish.1 = (f32[64,4096]{1,0:T(8,128)}, f32[8,8,128]{2,1,0:T(8,128)}, f32[1,1]{1,0:T(1,128)}) custom-call(f32[64,4096]{1,0:T(8,128)S(1)} %get-tuple-element.9.lo, f32[8,8,128]{2,1,0:T(8,128)S(1)} %get-tuple-element.10.fo, f32[1,1]{1,0:T(1,128)} %get-tuple-element.11.vo), custom_call_target="tpu_custom_call" | custom-call | tf_op jit(solution)/shard_map/finish/pallas_call | solution.py:341

commit v6 on v5

--- a/solution.py
+++ b/solution.py
@@ -55,7 +55,9 @@
 
     zhpeer = ((1 - zh) * 4 + x, pi)
 
-    small = [pltpu.make_async_copy(f_hbm, f, ssem.at[0]), pltpu.make_async_copy(lt_hbm, lt, ssem.at[1]),
+    first, rest = pl.ds(0, CH), pl.ds(CH, CT - CH)
+    late = pltpu.make_async_copy(lt_hbm.at[:, rest], lt.at[:, rest], ssem.at[4])
+    small = [pltpu.make_async_copy(f_hbm, f, ssem.at[0]), pltpu.make_async_copy(lt_hbm.at[:, first], lt.at[:, first], ssem.at[1]),
              pltpu.make_async_copy(b_hbm, bv, ssem.at[2]), pltpu.make_async_copy(w_hbm, w_ref, ssem.at[3])]
     for c in small:
         c.start()
@@ -68,6 +70,7 @@
     for i in range(AHEAD):
         for c in piece(i):
             c.start()
+    late.start()
     barrier = pltpu.get_barrier_semaphore()
     peers = [mate] + [ypeer(j)[1] for j in range(1, 4)] + [xpeer(j)[1] for j in range(1, 4)] + [ringpeer(j) for j in range(1, 8)]
     for dev in peers:
@@ -76,9 +79,7 @@
     row = lax.broadcasted_iota(jnp.int32, (16, 1024), 0)
     f3[64:80, :] = jnp.where(row < 3, 1.0, 0.0).astype(BF)
     v[...] = jnp.zeros_like(v)
-    gall[pl.ds(0, R), :] = jnp.zeros((R, 1024), BF)
-    for c in small:
-        c.wait()
+    small[0].wait()
     for t in range(8):
         h, m, l = split3(f[t].astype(F32) * LOG2E)
         sl = slice(t * 128, (t + 1) * 128)
@@ -86,6 +87,8 @@
         f3[128:192, sl] = m
         f3[192:256, sl] = l
         f2[:, sl] = f[t]
+    for c in small[1:]:
+        c.wait()
     wneg = [-math.log(2.0) * w_ref[t] for t in range(8)]
 
     def ydot(j, yy):
@@ -208,6 +211,7 @@
     at = {2: [(core_out, 0)], 3: [(y_out, 0)], 4: [(core_out, 1)], 5: [(y_out, 1)], 6: [(core_out, 2), (z_out, 0)], 7: [(y_out, 2)]}
 
     ydot(0, ya)
+    late.wait()
 
     def body(n, _):
         @pl.when(n < NB // 2 - AHEAD)
@@ -279,7 +283,7 @@
     for j in range(1, 8):
         vzcopy(j).wait_recv()
     a = ((vz[0] + vz[1]) + (vz[2] + vz[3])) + ((vz[4] + vz[5]) + (vz[6] + vz[7]))
-    vo_ref[...] = jnp.sum(a, axis=(0, 1), keepdims=True) * scale_v
+    vo_ref[...] = jnp.broadcast_to(jnp.sum(a, axis=(0, 1), keepdims=True) * scale_v, (8, 128))
     fzcopy.wait_recv()
     a = (fz[zh] + fz[2]) * scale_f
     for t in range(8):
@@ -304,9 +308,11 @@
         dcopy(i).wait_send()
 
 
-def finish(lo, fo, vo, lo_ref, fo_ref, vo_ref, sem):
-    copies = [pltpu.make_async_copy(lo.at[pl.ds(8 * i, 8)], lo_ref.at[pl.ds(8 * i, 8)], sem.at[i]) for i in range(8)]
-    copies += [pltpu.make_async_copy(fo, fo_ref, sem.at[8]), pltpu.make_async_copy(vo, vo_ref, sem.at[9])]
+def finish(lo, fo, vo, lo_ref, fo_ref, vo_ref, one, sem):
+    one[...] = vo[0:1, 0:1]
+    copies = [pltpu.make_async_copy(one, vo_ref, sem.at[9])]
+    copies += [pltpu.make_async_copy(lo.at[pl.ds(8 * i, 8)], lo_ref.at[pl.ds(8 * i, 8)], sem.at[i]) for i in range(8)]
+    copies += [pltpu.make_async_copy(fo, fo_ref, sem.at[8])]
     for c in copies:
         c.start()
     for c in copies:
@@ -325,14 +331,14 @@
         functools.partial(kernel, *scales),
         in_specs=[H] * 6,
         out_specs=[pl.BlockSpec(memory_space=V)] * 3,
-        out_shape=shapes,
+        out_shape=shapes[:2] + [jax.ShapeDtypeStruct((8, 128), F32)],
         scratch_shapes=[
             V((CT, 8, 128), BF), V((CT, 128), jnp.int32), V((1, CT), F32), V((64, CT), BF), V((8, 64, 128), BF),
             V((256, 1024), BF), V((64, 1024), BF), V((R, 1024), F32), V((R, 1024), F32), V((R * 8, 128), F32), V((CT, 1024), BF),
             V((2, 4, 8, 1024), F32), V((64, CT), F32), V((8, 128), F32),
             V((32, CT), F32), V((4, 8, CT), F32), V((4, 8, CT), F32),
             V((4, 2, 8, 1024), F32), V((3, 8, 1024), F32), V((8, 128), F32), V((4, 8, 128), F32), V((4, 8, 128), F32), V((8, 8, 128), F32),
-            pltpu.SMEM((8,), F32), D((2, NB // 2)), D((4,)), D((4,)), D((4,)), D((4, 4)), D((4, 4)), D((4, 4)), D((4, 4)), D((4, 4)), D((4, 4)), D((4,)), D((4,)),
+            pltpu.SMEM((8,), F32), D((2, NB // 2)), D((5,)), D((4,)), D((4,)), D((4, 4)), D((4, 4)), D((4, 4)), D((4, 4)), D((4, 4)), D((4, 4)), D((4,)), D((4,)),
             D((4,)), D((4,)), D((16,)), D((16,))],
         compiler_params=pltpu.CompilerParams(collective_id=0, has_side_effects=True, vmem_limit_bytes=44 << 20),
         name="adjoint",
@@ -340,10 +346,10 @@
     lo, fo, vo = (pltpu.with_memory_space_constraint(a, pltpu.VMEM) for a in (lo, fo, vo))
     lo, fo, vo = pl.pallas_call(
         finish,
-        in_specs=[A, A, A],
+        in_specs=[A, A, pl.BlockSpec(memory_space=V)],
         out_specs=[H, H, H],
         out_shape=shapes,
-        scratch_shapes=[D((10,))],
+        scratch_shapes=[V((1, 1), F32), D((10,))],
         name="finish",
     )(lo, fo, vo)
     return vo[0, 0], lo.T, fo

time: 40.8 us -> 39.7 us (0.973)
  Pallas kernels: 40.1 us -> 38.9 us
    pallas_call x1, Pallas kernels: 1.68 us -> 1.05 us  [per_device(): pl.pallas_call(finish, in_specs=[A, A, pl.BlockSpec(memory_space=V)], out...]
    pallas_call x1, Pallas kernels: 38.4 us -> 37.9 us  [per_device(): pl.pallas_call(functools.partial(kernel, *scales), in_specs=[H] * 6, out_...]
where the time goes in v6:
time: 39.7 us; the launch traced here: 39.6 us
  Pallas kernels  38.9 us (98%)
  between operations  0.64 us (2%)
    pallas_call x1, Pallas kernels, per_device(): pl.pallas_call(functools.partial(kernel, *scales), in_specs=[H] * 6, out_...  37.9 us
    pallas_call x1, Pallas kernels, per_device(): pl.pallas_call(finish, in_specs=[A, A, pl.BlockSpec(memory_space=V)], out...  1.05 us

profile of v6, /device:TPU:1, one launch (start us, length us, event | category | flops | bytes accessed | tf_op | source)
XLA Modules:
  0.0 39.6 jit_solution(16902510069334101299)
XLA Ops:
  0.6 37.9 %adjoint.1 = (f32[64,4096]{1,0:T(8,128)S(1)}, f32[8,8,128]{2,1,0:T(8,128)S(1)}, f32[8,128]{1,0:T(8,128)S(1)}) custom-call(bf16[4096,8,128]{2,1,0:T(8,128)(2,1)} %e_hbm.1, s32[4096,128]{1,0:T(8,128)} %d_hbm.1, f32[1,4096]{1,0:T(1,128)} %bitcast.5, bf16[64,4096]{1,0:T(8,128)(2,1)} %bitcast.4, bf16[8,64,128]{2,1,0:T(8,128)(2,1)} %f_hbm.1, f32[8]{0:T(128)} %w_hbm.1), custom_call_target="tpu_custom_call" | custom-call | tf_op jit(solution)/shard_map/adjoint/pallas_call | solution.py:330
  38.5 1.1 %finish.1 = (f32[64,4096]{1,0:T(8,128)}, f32[8,8,128]{2,1,0:T(8,128)}, f32[1,1]{1,0:T(1,128)}) custom-call(f32[64,4096]{1,0:T(8,128)S(1)} %get-tuple-element.9.lo, f32[8,8,128]{2,1,0:T(8,128)S(1)} %get-tuple-element.10.fo, f32[8,128]{1,0:T(8,128)S(1)} %get-tuple-element.11.vo), custom_call_target="tpu_custom_call" | custom-call | tf_op jit(solution)/shard_map/finish/pallas_call | solution.py:347

commit v7 on v6

--- a/solution.py
+++ b/solution.py
@@ -280,29 +280,28 @@
     d_out(0)
     a_out(3)
     d_out(1)
+    vcopy.wait_send()
+    for j in range(1, 4):
+        vycopy(j).wait_send()
+        vxcopy(j).wait_send()
+        fcopy(j).wait_send()
+    for i in range(4):
+        ccopy(i).wait_send()
+        for j in range(1, 4):
+            ycopy(i, j).wait_send()
+            zcopy(i, j).wait_send()
     for j in range(1, 8):
-        vzcopy(j).wait_recv()
+        vzcopy(j).wait()
     a = ((vz[0] + vz[1]) + (vz[2] + vz[3])) + ((vz[4] + vz[5]) + (vz[6] + vz[7]))
     vo_ref[...] = jnp.broadcast_to(jnp.sum(a, axis=(0, 1), keepdims=True) * scale_v, (8, 128))
-    fzcopy.wait_recv()
+    fzcopy.wait()
     a = (fz[zh] + fz[2]) * scale_f
     for t in range(8):
         fo_ref[t] = a[:, t * 128:(t + 1) * 128]
     d_out(2)
     d_out(3)
-    vcopy.wait_send()
-    fzcopy.wait_send()
-    for j in range(1, 4):
-        vycopy(j).wait_send()
-        vxcopy(j).wait_send()
-        fcopy(j).wait_send()
-    for j in range(1, 8):
-        vzcopy(j).wait_send()
     for i in range(4):
-        ccopy(i).wait_send()
-        for j in range(1, 4):
-            ycopy(i, j).wait_send()
-            zcopy(i, j).wait_send()
+        for j in range(1, 4):
             acopy(i, j).wait_send()
         dcopy(i).wait_recv()
         dcopy(i).wait_send()

time: 39.7 us -> 39.7 us (level)
  no operation moved by 1% of the time
where the time goes in v7:
time: 39.7 us; the launch traced here: 39.6 us
  Pallas kernels  38.9 us (98%)
  between operations  0.64 us (2%)
    pallas_call x1, Pallas kernels, per_device(): pl.pallas_call(functools.partial(kernel, *scales), in_specs=[H] * 6, out_...  37.9 us
    pallas_call x1, Pallas kernels, per_device(): pl.pallas_call(finish, in_specs=[A, A, pl.BlockSpec(memory_space=V)], out...  1.05 us

profile of v7, /device:TPU:1, one launch (start us, length us, event | category | flops | bytes accessed | tf_op | source)
XLA Modules:
  0.0 39.6 jit_solution(2709169791740151195)
XLA Ops:
  0.6 37.9 %adjoint.1 = (f32[64,4096]{1,0:T(8,128)S(1)}, f32[8,8,128]{2,1,0:T(8,128)S(1)}, f32[8,128]{1,0:T(8,128)S(1)}) custom-call(bf16[4096,8,128]{2,1,0:T(8,128)(2,1)} %e_hbm.1, s32[4096,128]{1,0:T(8,128)} %d_hbm.1, f32[1,4096]{1,0:T(1,128)} %bitcast.5, bf16[64,4096]{1,0:T(8,128)(2,1)} %bitcast.4, bf16[8,64,128]{2,1,0:T(8,128)(2,1)} %f_hbm.1, f32[8]{0:T(128)} %w_hbm.1), custom_call_target="tpu_custom_call" | custom-call | tf_op jit(solution)/shard_map/adjoint/pallas_call | solution.py:329
  38.5 1.1 %finish.1 = (f32[64,4096]{1,0:T(8,128)}, f32[8,8,128]{2,1,0:T(8,128)}, f32[1,1]{1,0:T(1,128)}) custom-call(f32[64,4096]{1,0:T(8,128)S(1)} %get-tuple-element.9.lo, f32[8,8,128]{2,1,0:T(8,128)S(1)} %get-tuple-element.10.fo, f32[8,128]{1,0:T(8,128)S(1)} %get-tuple-element.11.vo), custom_call_target="tpu_custom_call" | custom-call | tf_op jit(solution)/shard_map/finish/pallas_call | solution.py:346
